TPU v7x, 32 devices: a whole 2x2x4 slice. The times are simulated.
32 devices in a mesh: prow: 4 (over y, core), pcol: 8 (over z, x).
Axes of the slice: x: 2, y: 2, z: 4, core: 2. Of those that a mesh axis runs over, the one named last changes fastest.
Arguments:
- diag_one: float32 [1024, 1024], P('pcol')
- top_rows: bfloat16 [1024, 1024], P('pcol'), may hold values from -0.1875 to 0.1875
- panel_one: bfloat16 [16384, 1024], P(('prow', 'pcol')), may hold values from -6 to 6
- first_block: int32 [64], P(('prow', 'pcol')), may hold values from 0 to 3
- target: int32 [64], P(('prow', 'pcol')), may hold values from 0 to 63, as said below
- diag_two: float32 [1024, 1024], P('pcol'), may hold values from -6 to 6
- panel_two: bfloat16 [16384, 1024], P(('prow', 'pcol')), may hold values from -6 to 6
Outputs:
- panel_factor: bfloat16 [16384, 1024], P(('prow', 'pcol'))
- top_factor: bfloat16 [1024, 1024], P('pcol')
- diag_next: float32 [1024, 1024], P('pcol')
- panel_next: float32 [16384, 1024], P(('prow', 'pcol'))
Inputs may be any that keep to these rules, and one draw needn't show every extreme that they name: Row block t of the second supernode is held by grid row (t // 2) // 8 and grid column (t // 2) % 8; target[i] lies in the grid column of row block i; the 2 row blocks of one device go to 2 different grid rows; in every grid column one grid row receives a row block from every grid row.
All inputs are finite; a program needn't handle non-finite values.
Results may differ from a plain program's by a relative error of at most 0.0021.
Values may be sent and summed in bfloat16 or wider, within the bound.
No kernel may reach another device: no remote copies, remote signals or barrier semaphores. Data moves between devices by JAX's collectives and lax.ppermute only.
A program may use at most 128 MiB of HBM per device.

v0:
```python
import functools

import jax
import jax.numpy as jnp
from jax import lax
from jax.experimental import pallas as pl
from jax.experimental.pallas import tpu as pltpu
from jax.sharding import PartitionSpec as P

NB = 128
SUB = 32
VMEM = pl.BlockSpec(memory_space=pltpu.VMEM)


def split3(x):
    hi = x.astype(jnp.bfloat16)
    rest = x - hi.astype(jnp.float32)
    mid = rest.astype(jnp.bfloat16)
    low = (rest - mid.astype(jnp.float32)).astype(jnp.bfloat16)
    return hi, mid, low


def left_terms(x):
    hi, mid, low = split3(x)
    return jnp.concatenate([hi, hi, mid, hi, low, mid], 0)


def right_terms(x):
    hi, mid, low = split3(x)
    return jnp.concatenate([hi, mid, hi, low, hi, mid], 0)


def dot_tn(left, right):
    return lax.dot_general(
        left, right, (((0,), (0,)), ((), ())), preferred_element_type=jnp.float32
    )


def dot_nt(left, right):
    return lax.dot_general(
        left, right, (((1,), (1,)), ((), ())), preferred_element_type=jnp.float32
    )


def lanes(x, column, width):
    return jnp.broadcast_to(x[:, column : column + 1], (x.shape[0], width))


def wide(x, width):
    return jnp.tile(x, (1, width // x.shape[1]))


def eliminate(rows, base):
    width = rows[0].shape[1]
    groups = len(rows)
    rows = list(rows)
    done = []
    sublane = lax.broadcasted_iota(jnp.int32, (8, width), 0)
    for q in range(groups):
        first = base + 8 * q
        cols = [lanes(rows[q], first + c, NB) for c in range(8)]
        entry = {}
        for c in range(8):
            for i in range(c, 8):
                entry[i, c] = jnp.broadcast_to(cols[c][i : i + 1, :], (8, NB))
        row = [jnp.broadcast_to(rows[q][i : i + 1, :], (8, width)) for i in range(8)]
        below = [
            [lanes(rows[p], first + c, NB) for c in range(8)] for p in range(q + 1, groups)
        ]
        scale = []
        for j in range(8):
            pivot = entry[j, j]
            inverse = 1.0 / pivot
            scale.append(lax.rsqrt(pivot))
            ratio = {c: entry[c, j] * inverse for c in range(j + 1, 8)}
            for c in range(j + 1, 8):
                for i in range(c, 8):
                    entry[i, c] = entry[i, c] - entry[i, j] * ratio[c]
                row[c] = row[c] - wide(ratio[c], width) * row[j]
            for part in below:
                for c in range(j + 1, 8):
                    part[c] = part[c] - part[j] * ratio[c]
        final = [row[i] * wide(scale[i], width) for i in range(8)]
        merged = final[0]
        for i in range(1, 8):
            merged = jnp.where(sublane == i, final[i], merged)
        done.append(merged)
        for p, part in enumerate(below):
            for c in range(8):
                rows[q + 1 + p] = rows[q + 1 + p] - wide(part[c] * scale[c], width) * final[c]
    return done


def factor_block(block):
    rows = [block[8 * i : 8 * i + 8] for i in range(NB // 8)]
    step = SUB // 8
    done = []
    for b in range(NB // SUB):
        part = eliminate(rows[b * step : (b + 1) * step], b * SUB)
        done += part
        if (b + 1) * SUB < NB:
            solved = jnp.concatenate(part, 0)
            change = dot_tn(left_terms(solved[:, (b + 1) * SUB : NB]), right_terms(solved))
            for p in range((b + 1) * step, NB // 8):
                k = p - (b + 1) * step
                rows[p] = rows[p] - change[8 * k : 8 * k + 8]
    return jnp.concatenate(done, 0)


def factor_kernel(diag_ref, hi_ref, lo_ref, work, block, left, right):
    size = diag_ref.shape[0]
    count = size // NB
    work[...] = diag_ref[...]
    same = lax.broadcasted_iota(jnp.int32, (NB, NB), 0) == lax.broadcasted_iota(
        jnp.int32, (NB, NB), 1
    )
    unit = same.astype(jnp.float32)

    def step(k, carry):
        here = pl.ds(pl.multiple_of(k * NB, NB), NB)
        block[:, :NB] = work[here, here]
        block[:, NB:] = unit
        block[...] = factor_block(block[...])
        inverse = block[:, NB:]
        solved = dot_tn(left_terms(inverse.T), right_terms(work[here, :]))
        work[here, :] = solved
        work[here, here] = inverse
        solved = work[here, :]
        left[...] = left_terms(solved)
        right[...] = right_terms(solved)

        def update(i, inner):
            there = pl.ds(pl.multiple_of(i * NB, NB), NB)
            work[there, here] = jnp.zeros((NB, NB), jnp.float32)
            work[there, :] = work[there, :] - dot_tn(left[:, there], right[...])
            return inner

        lax.fori_loop(k + 1, count, update, 0)
        return carry

    lax.fori_loop(0, count, step, 0)

    def finish(k, carry):
        here = pl.ds(pl.multiple_of(k * NB, NB), NB)
        keep = lax.broadcasted_iota(jnp.int32, (NB, size), 1) <= (
            lax.broadcasted_iota(jnp.int32, (NB, size), 0) + k * NB
        )
        value = jnp.where(keep, work[here, :], 0.0)
        hi = value.astype(jnp.bfloat16)
        hi_ref[here, :] = hi
        lo_ref[here, :] = (value - hi.astype(jnp.float32)).astype(jnp.bfloat16)
        return carry

    lax.fori_loop(0, count, finish, 0)


def inverse_factor(diag):
    size = diag.shape[0]
    half = jax.ShapeDtypeStruct((size, size), jnp.bfloat16)
    return pl.pallas_call(
        factor_kernel,
        out_shape=(half, half),
        in_specs=[VMEM],
        out_specs=(VMEM, VMEM),
        scratch_shapes=[
            pltpu.VMEM((size, size), jnp.float32),
            pltpu.VMEM((NB, 2 * NB), jnp.float32),
            pltpu.VMEM((6 * NB, size), jnp.bfloat16),
            pltpu.VMEM((6 * NB, size), jnp.bfloat16),
        ],
        compiler_params=pltpu.CompilerParams(vmem_limit_bytes=40 * 2**20),
        cost_estimate=pl.CostEstimate(
            flops=2 * 6 * size**3, bytes_accessed=8 * size * size, transcendentals=0
        ),
        name="inverse_factor",
    )(diag)


def solve_rows(x, hi_ref, lo_ref):
    size = hi_ref.shape[0]
    width = 256
    parts = []
    for j in range(size // width):
        rows, upto = slice(j * width, (j + 1) * width), (j + 1) * width
        parts.append(
            dot_nt(x[:, :upto], hi_ref[rows, :upto]) + dot_nt(x[:, :upto], lo_ref[rows, :upto])
        )
    return jnp.concatenate(parts, 1).astype(jnp.bfloat16)


def apply_kernel(
    rows_b,
    index_ref,
    hi_ref,
    lo_ref,
    top_ref,
    own_ref,
    incoming_ref,
    diag_ref,
    panel_ref,
    factor_out,
    top_out,
    diag_out,
    panel_out,
    top_all,
):
    size = hi_ref.shape[0]
    local = top_out.shape[0]

    def block_of(i):
        return pl.ds(pl.multiple_of(i * rows_b, rows_b), rows_b)

    def do_top(i, carry):
        top_all[block_of(i), :] = solve_rows(top_ref[block_of(i), :], hi_ref, lo_ref)
        return carry

    def do_own(i, carry):
        factor_out[block_of(i), :] = solve_rows(own_ref[block_of(i), :], hi_ref, lo_ref)
        return carry

    lax.fori_loop(0, size // rows_b, do_top, 0)
    lax.fori_loop(0, own_ref.shape[0] // rows_b, do_own, 0)
    mine = top_all[pl.ds(pl.multiple_of(index_ref[0] * local, local), local), :]
    top_out[...] = mine
    diag_out[...] = diag_ref[...] - dot_nt(mine, top_all[...])
    panel_out[...] = panel_ref[...].astype(jnp.float32)

    def do_update(i, carry):
        solved = solve_rows(incoming_ref[block_of(i), :], hi_ref, lo_ref)
        change = dot_nt(solved, top_all[...]).astype(jnp.bfloat16)
        slot = block_of(jnp.maximum(index_ref[1 + i], 0))
        panel_out[slot, :] = panel_out[slot, :] - change.astype(jnp.float32)
        return carry

    lax.fori_loop(0, incoming_ref.shape[0] // rows_b, do_update, 0)


def apply_factor(rows_b, index, hi, lo, top, own, incoming, diag_two, panel_two):
    size = hi.shape[0]
    return pl.pallas_call(
        functools.partial(apply_kernel, rows_b),
        out_shape=(
            jax.ShapeDtypeStruct(own.shape, jnp.bfloat16),
            jax.ShapeDtypeStruct(diag_two.shape, jnp.bfloat16),
            jax.ShapeDtypeStruct(diag_two.shape, jnp.float32),
            jax.ShapeDtypeStruct(panel_two.shape, jnp.float32),
        ),
        in_specs=[pl.BlockSpec(memory_space=pltpu.SMEM)] + [VMEM] * 7,
        out_specs=(VMEM,) * 4,
        scratch_shapes=[pltpu.VMEM((size, size), jnp.bfloat16)],
        compiler_params=pltpu.CompilerParams(vmem_limit_bytes=48 * 2**20),
        cost_estimate=pl.CostEstimate(
            flops=2 * size * size * (3 * incoming.shape[0] + 3 * size),
            bytes_accessed=16 * size * size,
            transcendentals=0,
        ),
        name="apply_factor",
    )(index, hi, lo, top, own, incoming, diag_two, panel_two)


def on_device(diag_one, top_rows, panel_one, first_block, target, diag_two, panel_two):
    col_count = diag_one.shape[1]
    blocks = first_block.shape[0]
    block_rows = panel_one.shape[0] // blocks
    grid_rows = lax.axis_size("prow")
    grid_cols = lax.axis_size("pcol")
    whole_diag = lax.all_gather(diag_one, "pcol", axis=0, tiled=True)
    whole_top = lax.all_gather(top_rows, "pcol", axis=0, tiled=True)

    columns = jnp.arange(col_count, dtype=jnp.int32) // block_rows
    keep = columns[None, :] >= first_block[:, None]
    stacked = panel_one.reshape(blocks, block_rows, col_count)
    masked = jnp.where(keep[:, None, :], stacked, jnp.zeros_like(stacked))

    dest_row = target // (blocks * grid_cols)
    dest_slot = target % blocks
    routing = dest_row[None, :] == jnp.arange(grid_rows, dtype=jnp.int32)[:, None]
    send_slot = jnp.sum(jnp.where(routing, dest_slot[None, :] + 1, 0), axis=1) - 1
    outgoing = jnp.zeros((grid_rows, block_rows, col_count), jnp.bfloat16)
    for r in range(blocks):
        outgoing = jnp.where(routing[:, r, None, None], masked[r][None], outgoing)
    incoming = lax.all_to_all(outgoing, "prow", split_axis=0, concat_axis=0, tiled=True)
    incoming_slot = lax.all_to_all(send_slot, "prow", split_axis=0, concat_axis=0, tiled=True)
    index = jnp.concatenate(
        [lax.axis_index("pcol").astype(jnp.int32)[None], incoming_slot]
    )

    hi, lo = inverse_factor(whole_diag)
    panel_factor, top_own, diag_next, panel_next = apply_factor(
        block_rows,
        index,
        hi,
        lo,
        whole_top,
        masked.reshape(blocks * block_rows, col_count),
        incoming.reshape(grid_rows * block_rows, col_count),
        diag_two,
        panel_two,
    )
    return (panel_factor, top_own, diag_next, panel_next)


def solution(mesh):
    in_specs = (
        P("pcol", None),
        P("pcol", None),
        P(("prow", "pcol"), None),
        P(("prow", "pcol")),
        P(("prow", "pcol")),
        P("pcol", None),
        P(("prow", "pcol"), None),
    )
    out_specs = (
        P(("prow", "pcol"), None),
        P("pcol", None),
        P("pcol", None),
        P(("prow", "pcol"), None),
    )
    return jax.shard_map(
        on_device, mesh=mesh, in_specs=in_specs, out_specs=out_specs, check_vma=False
    )
```

profile of v0, /device:TPU:0, one launch (start us, length us, event | category | flops | bytes accessed | tf_op | source)
XLA Modules:
  0.0 168.3 jit_solution(7227586301203990555)
XLA Ops:
  7.2 0.0 all-gather.3.cloned.1.call-start
  7.2 0.7 all-gather.3.cloned.1.call-update
  7.9 0.0 all-gather.5.cloned.1.call-start
  7.9 0.7 all-gather.5.cloned.1.call-update
  8.6 0.7 and_select_fusion.1
  9.3 0.1 select_reduce_fusion
  9.4 0.7 copy.12
  10.1 4.3 %all-to-all-start = ((s32[4,1,1]{2,1,0:T(1,128)}), s32[4,1,1]{2,1,0:T(1,128)S(1)}, u32[]{:S(2)}, u32[]{:S(2)}) async-start(s32[4,1,1]{2,1,0:T(1,128)} %copy.12), calls=%async_computation | async-start | bytes 4096 | tf_op jit(solution)/shard_map/all_to_all | solution.py:283
  14.3 0.1 iota_compare_fusion
  14.4 0.7 broadcast_compare_fusion
  15.1 1.3 broadcast_select_fusion
  16.5 0.1 slice_bitcast_fusion.1
  16.5 1.7 %select_select_fusion = bf16[4,256,1024]{2,1,0:T(8,128)(2,1)} fusion(pred[4]{0:T(512)(128)(4,1)S(1)} %get-tuple-element.11, pred[4]{0:T(512)(128)(4,1)S(1)} %get-tuple-element.10, bf16[256,1024]{1,0:T(8,128)(2,1)S(1)} %get-tuple-element.9, bf16[256,1024]{1,0:T(8,128)(2,1)S(1)} %get-tuple-element.8), kind=kLoop, calls=%fused_computation | loop fusion | flops 2097152 | bytes 3145736 | tf_op jit(solution)/shard_map/jit(_where)/select_n | solution.py:281
  18.2 0.0 copy-start.6
  18.2 0.0 all-to-all-done
  18.2 4.6 %all-to-all-start.1 = ((bf16[4,256,1024]{2,1,0:T(8,128)(2,1)}), bf16[4,256,1024]{2,1,0:T(8,128)(2,1)}, u32[]{:S(2)}, u32[]{:S(2)}) async-start(bf16[4,256,1024]{2,1,0:T(8,128)(2,1)} %select_select_fusion), calls=%async_computation.1 | async-start | bytes 4194304 | tf_op jit(solution)/shard_map/all_to_all | solution.py:282
  22.9 0.0 copy-done.6
  22.9 0.1 bitcast_select_fusion.own_ref
  23.0 0.2 reduce
  23.1 0.1 pad_add_fusion.index_ref
  23.2 63.0 %all-gather.3.cloned.1.call-done.diag_ref = f32[1024,1024]{1,0:T(8,128)} async-done(((f32[128,1024]{1,0:T(8,128)}), f32[1024,1024]{1,0:T(8,128)}) %all-gather.3.cloned.1.call-update) | async-done | bytes 4194320 | tf_op jit(solution)/shard_map/all_gather | solution.py:267
  86.3 2.2 %copy-done = f32[1024,1024]{1,0:T(8,128)S(1)} copy-done((f32[1024,1024]{1,0:T(8,128)S(1)}, f32[1024,1024]{1,0:T(8,128)}, u32[]{:S(2)}) %copy-start) | copy-done | bytes 4194328
  88.4 51.2 %inverse_factor.1 = (bf16[1024,1024]{1,0:T(8,128)(2,1)S(1)}, bf16[1024,1024]{1,0:T(8,128)(2,1)S(1)}) custom-call(f32[1024,1024]{1,0:T(8,128)S(1)} %copy-done), custom_call_target="tpu_custom_call" | custom-call | flops 12884901888 | bytes 8388608 | tf_op jit(solution)/shard_map/inverse_factor/pallas_call | solution.py:160
  139.6 0.0 copy-start.3
  139.6 1.3 copy-done.3
  140.9 1.3 copy-done.5
  142.3 0.0 all-to-all-done.1
  142.3 0.0 copy-done.1
  142.3 0.0 copy-done.2
  142.3 0.0 copy-start.4
  142.3 1.6 copy-done.4
  143.9 17.6 %apply_factor.1 = (bf16[512,1024]{1,0:T(8,128)(2,1)}, bf16[128,1024]{1,0:T(8,128)(2,1)}, f32[128,1024]{1,0:T(8,128)}, f32[512,1024]{1,0:T(8,128)}) custom-call(s32[5]{0:T(128)S(1)} %pad_add_fusion.index_ref, bf16[1024,1024]{1,0:T(8,128)(2,1)S(1)} %copy-done.4, bf16[1024,1024]{1,0:T(8,128)(2,1)} %copy-done.5, ...), custom_call_target="tpu_custom_call" | custom-call | flops 12884901888 | bytes 16777216 | tf_op jit(solution)/shard_map/apply_factor/pallas_call | solution.py:240
  (8 shorter events, 0.0 us)
Async XLA Ops:
  7.2 79.1 %all-gather.3.cloned.1.call-start = ((), (), s32[]{:S(2)}) async-start(), calls=%async_computation.2 | async-start | bytes 4718592 | tf_op jit(solution)/shard_map/all_gather | solution.py:267
  7.9 134.4 %all-gather.5.cloned.1.call-start = ((), (), s32[]{:S(2)}) async-start(), calls=%async_computation.3 | async-start | bytes 2359296 | tf_op jit(solution)/shard_map/all_gather | solution.py:268
  10.1 8.2 %all-to-all-start = ((s32[4,1,1]{2,1,0:T(1,128)}), s32[4,1,1]{2,1,0:T(1,128)S(1)}, u32[]{:S(2)}, u32[]{:S(2)}) async-start(s32[4,1,1]{2,1,0:T(1,128)} %copy.12), calls=%async_computation | async-start | bytes 4096 | tf_op jit(solution)/shard_map/all_to_all | solution.py:283
  18.2 4.7 %copy-start.6 = (bf16[512,1024]{1,0:T(8,128)(2,1)S(1)}, bf16[512,1024]{1,0:T(8,128)(2,1)}, u32[]{:S(2)}) copy-start(bf16[512,1024]{1,0:T(8,128)(2,1)} %param.9) | copy-start | bytes 3145732
  18.2 124.0 %all-to-all-start.1 = ((bf16[4,256,1024]{2,1,0:T(8,128)(2,1)}), bf16[4,256,1024]{2,1,0:T(8,128)(2,1)}, u32[]{:S(2)}, u32[]{:S(2)}) async-start(bf16[4,256,1024]{2,1,0:T(8,128)(2,1)} %select_select_fusion), calls=%async_computation.1 | async-start | bytes 4194304 | tf_op jit(solution)/shard_map/all_to_all | solution.py:282
  86.3 2.2 %copy-start = (f32[1024,1024]{1,0:T(8,128)S(1)}, f32[1024,1024]{1,0:T(8,128)}, u32[]{:S(2)}) copy-start(f32[1024,1024]{1,0:T(8,128)} %all-gather.3.cloned.1.call-done.diag_ref) | copy-start | bytes 12582916
  88.4 53.8 %copy-start.1 = (bf16[512,1024]{1,0:T(8,128)(2,1)S(1)}, bf16[512,1024]{1,0:T(8,128)(2,1)}, u32[]{:S(2)}) copy-start(bf16[512,1024]{1,0:T(8,128)(2,1)} %panel_ref.1) | copy-start | bytes 3145732
  88.4 53.8 %copy-start.2 = (f32[128,1024]{1,0:T(8,128)S(1)}, f32[128,1024]{1,0:T(8,128)}, u32[]{:S(2)}) copy-start(f32[128,1024]{1,0:T(8,128)} %diag_ref.1) | copy-start | bytes 1572868
  139.6 1.3 copy-start.3
  140.9 1.3 copy-start.5
  142.3 1.6 copy-start.4
Sparse Core Ops, SparseCore 0:
  10.1 76.0 all-gather.2
  88.4 47.4 all-gather.4
where the time goes:
time: 169 us; the launch traced here: 168 us
  Pallas kernels  68.7 us (41%)
  waiting for transfers between devices  64.4 us (38%)
  between operations  14.1 us (8%)
  starting transfers between devices  8.96 us (5%)
  local copies, waits for them, and re-layouts  7.18 us (4%)
  other arithmetic  4.87 us (3%)
    all_gather x1, waiting for transfers between devices, on_device(): whole_diag = lax.all_gather(diag_one, 'pcol', axis=0, tiled=True)  63 us
    pallas_call x1, Pallas kernels, inverse_factor(): pl.pallas_call(factor_kernel, out_shape=(half, half), in_specs=[VMEM], ou...  51.2 us
    pallas_call x1, Pallas kernels, apply_factor(): pl.pallas_call(functools.partial(apply_kernel, rows_b), out_shape=(jax.Sh...  17.6 us
    unnamed x14, local copies, waits for them, and re-layouts  6.43 us
    all_to_all x1, starting transfers between devices, on_device(): lax.all_to_all(outgoing, 'prow', split_axis=0, concat_axis=0, tiled=True)  4.63 us
    all_to_all x1, starting transfers between devices, on_device(): lax.all_to_all(send_slot, 'prow', split_axis=0, concat_axis=0, tiled=True)  4.26 us
  transfers between devices with their start and end apart: 4, of which 1 were waited for; matrix products, arithmetic and copies ran while one was open for 3% of the time, Pallas kernels for 30%

commit v1 on v0

--- a/solution.py
+++ b/solution.py
@@ -107,10 +107,36 @@
     return jnp.concatenate(done, 0)
 
 
-def factor_kernel(diag_ref, hi_ref, lo_ref, work, block, left, right):
-    size = diag_ref.shape[0]
+def assemble_pieces(place_ref, mine_ref, other_ref, work):
+    inner = 2
+    strips, half, width = mine_ref.shape
+    count = work.shape[0] // NB
+    for core, ref in enumerate((mine_ref, other_ref)):
+        for slot in range(strips):
+            strip = (place_ref[0] ^ (slot // inner)) * inner + (place_ref[1] ^ (slot % inner))
+            row = pl.multiple_of(strip * NB + (place_ref[2] ^ core) * half, half)
+            for d in range(width // NB):
+                column = pl.multiple_of(((strip + d) % count) * NB, NB)
+                work[pl.ds(row, half), pl.ds(column, NB)] = ref[slot, :, d * NB : (d + 1) * NB]
+    for i in range(count):
+        for j in range(i + width // NB, count):
+            here, there = slice(i * NB, (i + 1) * NB), slice(j * NB, (j + 1) * NB)
+            work[here, there] = work[there, here].T
+
+
+def factor_pieces_kernel(place_ref, mine_ref, other_ref, *rest):
+    assemble_pieces(place_ref, mine_ref, other_ref, rest[2])
+    factor_kernel(*rest)
+
+
+def factor_whole_kernel(diag_ref, *rest):
+    rest[2][...] = diag_ref[...]
+    factor_kernel(*rest)
+
+
+def factor_kernel(hi_ref, lo_ref, work, block, left, right):
+    size = work.shape[0]
     count = size // NB
-    work[...] = diag_ref[...]
     same = lax.broadcasted_iota(jnp.int32, (NB, NB), 0) == lax.broadcasted_iota(
         jnp.int32, (NB, NB), 1
     )
@@ -154,13 +180,12 @@
     lax.fori_loop(0, count, finish, 0)
 
 
-def inverse_factor(diag):
-    size = diag.shape[0]
+def inverse_factor(kernel, in_specs, size, operands):
     half = jax.ShapeDtypeStruct((size, size), jnp.bfloat16)
     return pl.pallas_call(
-        factor_kernel,
+        kernel,
         out_shape=(half, half),
-        in_specs=[VMEM],
+        in_specs=in_specs,
         out_specs=(VMEM, VMEM),
         scratch_shapes=[
             pltpu.VMEM((size, size), jnp.float32),
@@ -173,7 +198,39 @@
             flops=2 * 6 * size**3, bytes_accessed=8 * size * size, transcendentals=0
         ),
         name="inverse_factor",
-    )(diag)
+    )(*operands)
+
+
+def gather_and_factor(strip):
+    rows, size = strip.shape
+    count = lax.axis_size("pcol")
+    if rows != NB or count != 8:
+        whole = lax.all_gather(strip, "pcol", axis=0, tiled=True)
+        return inverse_factor(factor_whole_kernel, [VMEM], size, (whole,))
+    column = lax.axis_index("pcol")
+    outer, inner, core = column // 2, column % 2, lax.axis_index("prow") % 2
+    reach = (count // 2 + 1) * NB
+    piece = lax.dynamic_slice_in_dim(strip, core * (rows // 2), rows // 2, 0)
+    piece = lax.dynamic_slice_in_dim(
+        jnp.concatenate([piece, piece], 1), column * NB, reach, 1
+    )
+    got = [piece]
+    for s in range(1, count // 2):
+        got.append(
+            lax.ppermute(piece, "pcol", [(i, (i // 2 ^ s) * 2 + i % 2) for i in range(count)])
+        )
+    both = []
+    for part in got:
+        both += [part, lax.ppermute(part, "pcol", [(i, i ^ 1) for i in range(count)])]
+    mine = jnp.stack(both)
+    other = lax.ppermute(mine, "prow", [(i, i ^ 1) for i in range(lax.axis_size("prow"))])
+    place = jnp.stack([outer, inner, core]).astype(jnp.int32)
+    return inverse_factor(
+        factor_pieces_kernel,
+        [pl.BlockSpec(memory_space=pltpu.SMEM), VMEM, VMEM],
+        size,
+        (place, mine, other),
+    )
 
 
 def solve_rows(x, hi_ref, lo_ref):
@@ -264,7 +321,6 @@
     block_rows = panel_one.shape[0] // blocks
     grid_rows = lax.axis_size("prow")
     grid_cols = lax.axis_size("pcol")
-    whole_diag = lax.all_gather(diag_one, "pcol", axis=0, tiled=True)
     whole_top = lax.all_gather(top_rows, "pcol", axis=0, tiled=True)
 
     columns = jnp.arange(col_count, dtype=jnp.int32) // block_rows
@@ -285,7 +341,7 @@
         [lax.axis_index("pcol").astype(jnp.int32)[None], incoming_slot]
     )
 
-    hi, lo = inverse_factor(whole_diag)
+    hi, lo = gather_and_factor(diag_one)
     panel_factor, top_own, diag_next, panel_next = apply_factor(
         block_rows,
         index,

time: 169 us -> 133 us (0.79)
  the two profiles are of different devices: /device:TPU:0 before, /device:TPU:21 now
where the time goes in v1:
time: 133 us
  Pallas kernels  70.3 us (53%)
  starting transfers between devices  21.2 us (16%)
  waiting for transfers between devices  15.3 us (12%)
  between operations  14.2 us (11%)
  local copies, waits for them, and re-layouts  7.29 us (5%)
  other arithmetic  4.38 us (3%)
    pallas_call x1, Pallas kernels, inverse_factor(): pl.pallas_call(kernel, out_shape=(half, half), in_specs=in_specs, out_spe...  52.8 us
    pallas_call x1, Pallas kernels, apply_factor(): pl.pallas_call(functools.partial(apply_kernel, rows_b), out_shape=(jax.Sh...  17.6 us
    ppermute x3, waiting for transfers between devices, gather_and_factor(): lax.ppermute(piece, 'pcol', [(i, (i // 2 ^ s) * 2 + i % 2) for i in range...  10.8 us
    unnamed x24, local copies, waits for them, and re-layouts  6.52 us
    ppermute x1, starting transfers between devices, gather_and_factor(): lax.ppermute(mine, 'prow', [(i, i ^ 1) for i in range(lax.axis_size('prow...  6.24 us
    all_to_all x1, starting transfers between devices, on_device(): lax.all_to_all(send_slot, 'prow', split_axis=0, concat_axis=0, tiled=True)  5.13 us
    all_to_all x1, starting transfers between devices, on_device(): lax.all_to_all(outgoing, 'prow', split_axis=0, concat_axis=0, tiled=True)  4.43 us
    ppermute x4, waiting for transfers between devices, gather_and_factor(): lax.ppermute(part, 'pcol', [(i, i ^ 1) for i in range(count)])  4.42 us
  transfers between devices with their start and end apart: 11, of which 2 were waited for; matrix products, arithmetic and copies ran while one was open for 3% of the time, Pallas kernels for 40%

profile of v1, /device:TPU:21, one launch (start us, length us, event | category | flops | bytes accessed | tf_op | source)
XLA Modules:
  0.0 132.7 jit_solution(7138363899332704269)
XLA Ops:
  7.2 0.0 all-gather.2.cloned.1.call-start
  7.3 0.9 copy-done
  8.2 0.7 bitcast_dynamic-update-slice_fusion.7
  9.0 1.3 collective-permute-start.1
  10.2 1.2 collective-permute-start
  11.5 0.1 collective-permute-start.3
  11.5 1.3 collective-permute-start.5
  12.8 0.0 all-gather.2.cloned.1.call-update
  12.9 0.1 select_reduce_fusion
  13.0 0.7 copy.12
  13.6 5.1 %all-to-all-start = ((s32[4,1,1]{2,1,0:T(1,128)}), s32[4,1,1]{2,1,0:T(1,128)S(1)}, u32[]{:S(2)}, u32[]{:S(2)}) async-start(s32[4,1,1]{2,1,0:T(1,128)} %copy.12), calls=%async_computation | async-start | bytes 4096 | tf_op jit(solution)/shard_map/all_to_all | solution.py:339
  18.8 0.1 broadcast_compare_fusion
  18.8 0.1 iota_compare_fusion
  18.9 0.3 collective-permute-start.2
  19.2 1.2 collective-permute-start.4
  20.4 10.8 %collective-permute-done.5 = f32[64,640]{1,0:T(8,128)S(1)} collective-permute-done((f32[64,640]{1,0:T(8,128)}, f32[64,640]{1,0:T(8,128)S(1)}, u32[]{:S(2)}, u32[]{:S(2)}) %collective-permute-start.5) | collective-permute-done | bytes 163872 | tf_op jit(solution)/shard_map/ppermute | solution.py:220
  31.4 4.4 %collective-permute-done.6 = f32[64,640]{1,0:T(8,128)S(1)} collective-permute-done((f32[64,640]{1,0:T(8,128)S(1)}, f32[64,640]{1,0:T(8,128)S(1)}, u32[]{:S(2)}, u32[]{:S(2)}) %collective-permute-start.6) | collective-permute-done | bytes 163872 | tf_op jit(solution)/shard_map/ppermute | solution.py:224
  35.8 6.2 %collective-permute-start.7 = (f32[8,64,640]{2,1,0:T(8,128)S(1)}, f32[8,64,640]{2,1,0:T(8,128)}, u32[]{:S(2)}, u32[]{:S(2)}) collective-permute-start(f32[8,64,640]{2,1,0:T(8,128)S(1)} %bitcast_dynamic-update-slice_fusion.mine_ref), channel_id=1, source_target_pairs={{0,8},{8,0},{16,24},{24,16},{1,9},{9,1},{17,25},{25,17},{2,10},{10... | collective-permute-start | bytes 3932168 | tf_op jit(solution)/shard_map/ppermute | solution.py:226
  42.1 0.1 broadcast_select_fusion
  42.1 0.1 slice_bitcast_fusion.1
  42.2 1.7 %select_select_fusion = bf16[4,256,1024]{2,1,0:T(8,128)(2,1)} fusion(pred[4]{0:T(512)(128)(4,1)S(1)} %get-tuple-element.13, pred[4]{0:T(512)(128)(4,1)S(1)} %get-tuple-element.12, bf16[256,1024]{1,0:T(8,128)(2,1)S(1)} %get-tuple-element.11, bf16[256,1024]{1,0:T(8,128)(2,1)S(1)} %get-tuple-element.10), kind=kLoop, calls=%fused_computation | loop fusion | flops 2097152 | bytes 3145736 | tf_op jit(solution)/shard_map/jit(_where)/select_n | solution.py:337
  43.9 4.4 %all-to-all-start.1 = ((bf16[4,256,1024]{2,1,0:T(8,128)(2,1)}), bf16[4,256,1024]{2,1,0:T(8,128)(2,1)}, u32[]{:S(2)}, u32[]{:S(2)}) async-start(bf16[4,256,1024]{2,1,0:T(8,128)(2,1)} %select_select_fusion), calls=%async_computation.1 | async-start | bytes 4194304 | tf_op jit(solution)/shard_map/all_to_all | solution.py:338
  48.4 1.3 bitcast_select_fusion.own_ref
  49.7 0.1 pad_add_fusion.1.place_ref
  49.8 0.2 reduce
  50.0 0.1 pad_add_fusion.index_ref
  50.0 52.8 %inverse_factor.1 = (bf16[1024,1024]{1,0:T(8,128)(2,1)S(1)}, bf16[1024,1024]{1,0:T(8,128)(2,1)S(1)}) custom-call(s32[3]{0:T(128)S(1)} %pad_add_fusion.1.place_ref, f32[8,64,640]{2,1,0:T(8,128)S(1)} %bitcast_dynamic-update-slice_fusion.mine_ref, f32[8,64,640]{2,1,0:T(8,128)} %collective-permute-done.7.other_ref), custom_call_target="tpu_custom_call" | custom-call | flops 12884901888 | bytes 8388608 | tf_op jit(solution)/shard_map/inverse_factor/pallas_call | solution.py:185
  102.8 1.3 copy-done.3
  104.2 1.3 %copy-done.5 = bf16[1024,1024]{1,0:T(8,128)(2,1)} copy-done((bf16[1024,1024]{1,0:T(8,128)(2,1)}, bf16[1024,1024]{1,0:T(8,128)(2,1)S(1)}, u32[]{:S(2)}) %copy-start.5) | copy-done | bytes 2097176
  105.5 1.2 copy-done.1
  106.7 1.6 %copy-done.4 = bf16[1024,1024]{1,0:T(8,128)(2,1)S(1)} copy-done((bf16[1024,1024]{1,0:T(8,128)(2,1)S(1)}, bf16[1024,1024]{1,0:T(8,128)(2,1)}, u32[]{:S(2)}) %copy-start.4) | copy-done | bytes 2097176
  108.3 17.6 %apply_factor.1 = (bf16[512,1024]{1,0:T(8,128)(2,1)}, bf16[128,1024]{1,0:T(8,128)(2,1)}, f32[128,1024]{1,0:T(8,128)}, f32[512,1024]{1,0:T(8,128)}) custom-call(s32[5]{0:T(128)S(1)} %pad_add_fusion.index_ref, bf16[1024,1024]{1,0:T(8,128)(2,1)S(1)} %copy-done.4, bf16[1024,1024]{1,0:T(8,128)(2,1)} %copy-done.5, ...), custom_call_target="tpu_custom_call" | custom-call | flops 12884901888 | bytes 16777216 | tf_op jit(solution)/shard_map/apply_factor/pallas_call | solution.py:297
  (35 shorter events, 0.2 us)
Async XLA Ops:
  7.2 1.0 copy-start
  7.2 5.7 %copy-start.8 = (s32[2]{0:T(128)S(1)}, s32[2]{0:T(128)}, u32[]{:S(2)}) copy-start(s32[2]{0:T(128)} %param.11) | copy-start | bytes 28
  7.2 11.6 %copy-start.7 = (s32[2]{0:T(128)S(1)}, s32[2]{0:T(128)}, u32[]{:S(2)}) copy-start(s32[2]{0:T(128)} %param.10) | copy-start | bytes 28
  7.2 98.3 %all-gather.2.cloned.1.call-start = ((), (), s32[]{:S(2)}) async-start(), calls=%async_computation.2 | async-start | bytes 2359296 | tf_op jit(solution)/shard_map/all_gather | solution.py:324
  8.9 33.1 %copy-start.6 = (bf16[512,1024]{1,0:T(8,128)(2,1)S(1)}, bf16[512,1024]{1,0:T(8,128)(2,1)}, u32[]{:S(2)}) copy-start(bf16[512,1024]{1,0:T(8,128)(2,1)} %param.9) | copy-start | bytes 3145732
  9.0 10.0 %collective-permute-start.1 = (f32[64,640]{1,0:T(8,128)}, f32[64,640]{1,0:T(8,128)S(1)}, u32[]{:S(2)}, u32[]{:S(2)}) collective-permute-start(f32[64,640]{1,0:T(8,128)} %get-tuple-element.9), channel_id=1, source_target_pairs={{0,2},{1,3},{2,0},{3,1},{4,6},{5,7},{6,4},{7,5},{8,10},{9,11},{10,... | collective-permute-start | bytes 491528 | tf_op jit(solution)/shard_map/ppermute | solution.py:220
  10.2 21.0 %collective-permute-start = (f32[64,640]{1,0:T(8,128)}, f32[64,640]{1,0:T(8,128)S(1)}, u32[]{:S(2)}, u32[]{:S(2)}) collective-permute-start(f32[64,640]{1,0:T(8,128)} %get-tuple-element.9), channel_id=1, source_target_pairs={{0,1},{1,0},{2,3},{3,2},{4,5},{5,4},{6,7},{7,6},{8,9},{9,8},{10,11... | collective-permute-start | bytes 491528 | tf_op jit(solution)/shard_map/ppermute | solution.py:224
  11.5 7.7 %collective-permute-start.3 = (f32[64,640]{1,0:T(8,128)}, f32[64,640]{1,0:T(8,128)S(1)}, u32[]{:S(2)}, u32[]{:S(2)}) collective-permute-start(f32[64,640]{1,0:T(8,128)} %get-tuple-element.9), channel_id=1, source_target_pairs={{0,4},{1,5},{2,6},{3,7},{4,0},{5,1},{6,2},{7,3},{8,12},{9,13},{10,... | collective-permute-start | bytes 491528 | tf_op jit(solution)/shard_map/ppermute | solution.py:220
  11.5 19.7 %collective-permute-start.5 = (f32[64,640]{1,0:T(8,128)}, f32[64,640]{1,0:T(8,128)S(1)}, u32[]{:S(2)}, u32[]{:S(2)}) collective-permute-start(f32[64,640]{1,0:T(8,128)} %get-tuple-element.9), channel_id=1, source_target_pairs={{0,6},{1,7},{2,4},{3,5},{4,2},{5,3},{6,0},{7,1},{8,14},{9,15},{10,... | collective-permute-start | bytes 491528 | tf_op jit(solution)/shard_map/ppermute | solution.py:220
  13.6 30.3 %all-to-all-start = ((s32[4,1,1]{2,1,0:T(1,128)}), s32[4,1,1]{2,1,0:T(1,128)S(1)}, u32[]{:S(2)}, u32[]{:S(2)}) async-start(s32[4,1,1]{2,1,0:T(1,128)} %copy.12), calls=%async_computation | async-start | bytes 4096 | tf_op jit(solution)/shard_map/all_to_all | solution.py:339
  18.9 12.3 %collective-permute-start.2 = (f32[64,640]{1,0:T(8,128)S(1)}, f32[64,640]{1,0:T(8,128)S(1)}, u32[]{:S(2)}, u32[]{:S(2)}) collective-permute-start(f32[64,640]{1,0:T(8,128)S(1)} %collective-permute-done.1), channel_id=1, source_target_pairs={{0,1},{1,0},{2,3},{3,2},{4,5},{5,4},{6,7},{7,6},{8,9},{9,8},{10,11... | collective-permute-start | bytes 491528 | tf_op jit(solution)/shard_map/ppermute | solution.py:224
  19.2 12.1 %collective-permute-start.4 = (f32[64,640]{1,0:T(8,128)S(1)}, f32[64,640]{1,0:T(8,128)S(1)}, u32[]{:S(2)}, u32[]{:S(2)}) collective-permute-start(f32[64,640]{1,0:T(8,128)S(1)} %collective-permute-done.3), channel_id=1, source_target_pairs={{0,1},{1,0},{2,3},{3,2},{4,5},{5,4},{6,7},{7,6},{8,9},{9,8},{10,11... | collective-permute-start | bytes 491528 | tf_op jit(solution)/shard_map/ppermute | solution.py:224
  31.2 4.6 %collective-permute-start.6 = (f32[64,640]{1,0:T(8,128)S(1)}, f32[64,640]{1,0:T(8,128)S(1)}, u32[]{:S(2)}, u32[]{:S(2)}) collective-permute-start(f32[64,640]{1,0:T(8,128)S(1)} %collective-permute-done.5), channel_id=1, source_target_pairs={{0,1},{1,0},{2,3},{3,2},{4,5},{5,4},{6,7},{7,6},{8,9},{9,8},{10,11... | collective-permute-start | bytes 491528 | tf_op jit(solution)/shard_map/ppermute | solution.py:224
  35.8 14.2 %collective-permute-start.7 = (f32[8,64,640]{2,1,0:T(8,128)S(1)}, f32[8,64,640]{2,1,0:T(8,128)}, u32[]{:S(2)}, u32[]{:S(2)}) collective-permute-start(f32[8,64,640]{2,1,0:T(8,128)S(1)} %bitcast_dynamic-update-slice_fusion.mine_ref), channel_id=1, source_target_pairs={{0,8},{8,0},{16,24},{24,16},{1,9},{9,1},{17,25},{25,17},{2,10},{10... | collective-permute-start | bytes 3932168 | tf_op jit(solution)/shard_map/ppermute | solution.py:226
  43.9 61.6 %all-to-all-start.1 = ((bf16[4,256,1024]{2,1,0:T(8,128)(2,1)}), bf16[4,256,1024]{2,1,0:T(8,128)(2,1)}, u32[]{:S(2)}, u32[]{:S(2)}) async-start(bf16[4,256,1024]{2,1,0:T(8,128)(2,1)} %select_select_fusion), calls=%async_computation.1 | async-start | bytes 4194304 | tf_op jit(solution)/shard_map/all_to_all | solution.py:338
  50.0 55.5 %copy-start.2 = (f32[128,1024]{1,0:T(8,128)S(1)}, f32[128,1024]{1,0:T(8,128)}, u32[]{:S(2)}) copy-start(f32[128,1024]{1,0:T(8,128)} %diag_ref.1) | copy-start | bytes 1572868
  102.8 1.3 copy-start.3
  104.2 1.3 %copy-start.5 = (bf16[1024,1024]{1,0:T(8,128)(2,1)}, bf16[1024,1024]{1,0:T(8,128)(2,1)S(1)}, u32[]{:S(2)}) copy-start(bf16[1024,1024]{1,0:T(8,128)(2,1)S(1)} %get-tuple-element.7.lo_ref) | copy-start | bytes 6291460
  105.5 1.2 copy-start.1
  106.7 1.6 %copy-start.4 = (bf16[1024,1024]{1,0:T(8,128)(2,1)S(1)}, bf16[1024,1024]{1,0:T(8,128)(2,1)}, u32[]{:S(2)}) copy-start(bf16[1024,1024]{1,0:T(8,128)(2,1)} %copy-done.3) | copy-start | bytes 6291460
Sparse Core Ops, SparseCore 0:
  13.0 51.6 all-gather.1
